TPU v7x, 32 devices: a whole 2x2x4 slice. The times are simulated.
32 devices in a mesh: var: 2 (over x), tok: 16 (over z, y, core).
Axes of the slice: x: 2, y: 2, z: 4, core: 2. Of those that a mesh axis runs over, the one named last changes fastest.
Arguments:
- pixels: bfloat16 [16, 2048, 320], P('tok', None, 'var'), may hold values from -6 to 6
- w_embed: bfloat16 [320, 768], P('var'), may hold values from -0.3125 to 0.3125
- w_qkv: bfloat16 [768, 2304], replicated, may hold values from -0.21875 to 0.21875
- w_out: bfloat16 [768, 768], replicated, may hold values from -1.5 to 1.5
- w_up: bfloat16 [768, 3072], replicated, may hold values from -0.21875 to 0.21875
- w_down: bfloat16 [3072, 768], replicated, may hold values from -0.109375 to 0.109375
- w_head: bfloat16 [768, 320], replicated, may hold values from -0.21875 to 0.21875
- first_gain: float32 [768], replicated, may hold values from 0.25 to 1.75
- first_bias: float32 [768], replicated, may hold values from -4 to 4
- second_gain: float32 [768], replicated, may hold values from 0.25 to 1.75
- second_bias: float32 [768], replicated, may hold values from -4 to 4
- patch_cells: int32 [16, 2048], P('tok', 'var'), may hold values from 0 to 511, as said below
- field_ids: int32 [16, 2048], P('tok', 'var'), may hold values from 0 to 255, as said below
- visible: int32 [16, 2048], P('tok', 'var'), may hold values 0 or 1
- cotangent: bfloat16 [16, 2048, 320], P('tok', None, 'var'), may hold values from -6 to 6
Outputs:
- reconstruction: bfloat16 [16, 2048, 320], P('tok', None, 'var')
- pixel_grad: bfloat16 [16, 2048, 320], P('tok', None, 'var')
- w_embed_grad: float32 [320, 768], P('var')
- w_qkv_grad: float32 [768, 2304], P('tok')
- w_out_grad: float32 [768, 768], P('tok')
- w_up_grad: float32 [768, 3072], P('tok')
- w_down_grad: float32 [3072, 768], P('tok')
- w_head_grad: float32 [768, 320], P('tok')
- first_gain_grad: float32 [768], P('tok')
- first_bias_grad: float32 [768], P('tok')
- second_gain_grad: float32 [768], P('tok')
- second_bias_grad: float32 [768], P('tok')
Inputs may be any that keep to these rules, and one draw needn't show every extreme that they name: `field_ids`: each aligned slab of 512 rows holds either one field of 512 patches or 4 fields of 128 patches in a row; a field's id is 512 // 128 times its slab's number plus its place in the slab; the first slab holds one field of 512 patches, the last 4 fields of 128 patches. `patch_cells`: A field of 512 patches holds each cell r * 32 + c with r < 16, c < 32 once; a field of 128 patches each cell r * 32 + c with r < 8, c < 16 once; in any order.
All inputs are finite; a program needn't handle non-finite values. No bound on the sum of `visible` on one device may be relied on, other than what follows from the above.
Results may differ from a plain program's by a relative error of at most 0.025.
Values may be sent and summed in bfloat16 or wider, within the bound.
A program may use at most 256 MiB of HBM per device.

v0:
```python
import math

import jax
import jax.numpy as jnp
from jax import lax
from jax.sharding import PartitionSpec as P

HEADS = 12
HEAD_SIZE = 64
BIG = 512
BIG_COLS = 32


def layer_norm(inputs, norm_gain, norm_bias):
    center = inputs - jnp.mean(inputs, axis=-1, keepdims=True)
    variance = jnp.mean(center * center, axis=-1, keepdims=True)
    return center * lax.rsqrt(variance + 1e-06) * norm_gain + norm_bias


def gelu_exact(inputs):
    return jax.nn.gelu(inputs, approximate=False)


def place_table(cell_rows, model_width):
    quarter = model_width // 4
    ladder = jnp.arange(quarter).astype(jnp.float32) / quarter
    frequency = jnp.exp(-math.log(10000.0) * ladder)
    row_at = (cell_rows // BIG_COLS).astype(jnp.float32)[:, None] * frequency[None, :]
    col_at = (cell_rows % BIG_COLS).astype(jnp.float32)[:, None] * frequency[None, :]
    return jnp.concatenate(
        [jnp.sin(row_at), jnp.cos(row_at), jnp.sin(col_at), jnp.cos(col_at)], axis=1
    )


def dot_last(left, right):
    return lax.dot_general(
        left, right, (((1,), (1,)), ((), ())), preferred_element_type=jnp.float32
    )


def dot_first(left, right):
    return lax.dot_general(
        left, right, (((0,), (0,)), ((), ())), preferred_element_type=jnp.float32
    )


def slab_mask(id_rows, seen_rows):
    slab_ids = id_rows.reshape(-1, BIG)
    slab_seen = seen_rows.reshape(-1, BIG)
    diagonal = jnp.eye(BIG, dtype=bool)
    return (slab_ids[:, :, None] == slab_ids[:, None, :]) & (
        (slab_seen[:, None, :] == 1) | diagonal[None]
    )


def split_heads(qkv_rows):
    slab_count = qkv_rows.shape[0] // BIG
    shaped = qkv_rows.reshape(slab_count, BIG, 3, HEADS, HEAD_SIZE)
    return (shaped[:, :, 0], shaped[:, :, 1], shaped[:, :, 2])


def slab_scores(query_matrix, key_matrix, allowed):
    attention_scores = jnp.einsum(
        "snhd,smhd->shnm", query_matrix, key_matrix, preferred_element_type=jnp.float32
    ) * HEAD_SIZE ** (-0.5)
    return jnp.where(allowed[:, None], attention_scores, -1e30)


def attention_forward(qkv_rows, allowed):
    query_matrix, key_matrix, value_matrix = split_heads(qkv_rows)
    attention_scores = slab_scores(query_matrix, key_matrix, allowed)
    peak = jnp.max(attention_scores, axis=-1, keepdims=True)
    lifted = jnp.exp(attention_scores - peak)
    denominator = jnp.sum(lifted, axis=-1, keepdims=True)
    probability = (lifted / denominator).astype(jnp.bfloat16)
    attention_output = jnp.einsum(
        "shnm,smhd->snhd", probability, value_matrix, preferred_element_type=jnp.float32
    )
    log_total = peak[..., 0] + jnp.log(denominator[..., 0])
    return (
        attention_output.reshape(qkv_rows.shape[0], HEADS * HEAD_SIZE).astype(jnp.bfloat16),
        log_total,
    )


def attention_backward(qkv_rows, allowed, log_total, attended_grad):
    query_matrix, key_matrix, value_matrix = split_heads(qkv_rows)
    attention_scores = slab_scores(query_matrix, key_matrix, allowed)
    probability = jnp.exp(attention_scores - log_total[..., None])
    grad_shaped = attended_grad.reshape(query_matrix.shape)
    value_grad = jnp.einsum(
        "shnm,snhd->smhd",
        probability.astype(jnp.bfloat16),
        grad_shaped,
        preferred_element_type=jnp.float32,
    )
    prob_grad = jnp.einsum(
        "snhd,smhd->shnm", grad_shaped, value_matrix, preferred_element_type=jnp.float32
    )
    row_dot = jnp.sum(probability * prob_grad, axis=-1, keepdims=True)
    score_grad = (probability * (prob_grad - row_dot)).astype(jnp.bfloat16)
    query_grad = jnp.einsum(
        "shnm,smhd->snhd", score_grad, key_matrix, preferred_element_type=jnp.float32
    ) * HEAD_SIZE ** (-0.5)
    key_grad = jnp.einsum(
        "shnm,snhd->smhd", score_grad, query_matrix, preferred_element_type=jnp.float32
    ) * HEAD_SIZE ** (-0.5)
    stacked = jnp.stack([query_grad, key_grad, value_grad], axis=2)
    return stacked.reshape(qkv_rows.shape).astype(jnp.bfloat16)


def per_device(
    pixels,
    w_embed,
    w_qkv,
    w_out,
    w_up,
    w_down,
    w_head,
    first_gain,
    first_bias,
    second_gain,
    second_bias,
    patch_cells,
    field_ids,
    visible,
    cotangent,
):
    pixel_rows = pixels[0]
    cell_rows = patch_cells[0]
    id_rows = field_ids[0]
    seen_rows = visible[0]
    model_width = w_qkv.shape[0]
    embedded = lax.psum_scatter(
        jnp.dot(pixel_rows, w_embed, preferred_element_type=jnp.float32).astype(jnp.bfloat16),
        "var",
        scatter_dimension=0,
        tiled=True,
    ).astype(jnp.float32)
    start_rows = embedded + place_table(cell_rows, model_width)
    normed, first_pull = jax.vjp(layer_norm, start_rows, first_gain, first_bias)
    normed = normed.astype(jnp.bfloat16)
    qkv_rows = jnp.dot(normed, w_qkv, preferred_element_type=jnp.float32).astype(jnp.bfloat16)
    allowed = slab_mask(id_rows, seen_rows)
    attention_output, log_total = attention_forward(qkv_rows, allowed)
    middle = start_rows + jnp.dot(attention_output, w_out, preferred_element_type=jnp.float32)
    normed_two, second_pull = jax.vjp(layer_norm, middle, second_gain, second_bias)
    normed_two = normed_two.astype(jnp.bfloat16)
    hidden = jnp.dot(normed_two, w_up, preferred_element_type=jnp.float32)
    activated, gelu_pull = jax.vjp(gelu_exact, hidden)
    activated_low = activated.astype(jnp.bfloat16)
    final_rows = (
        middle + jnp.dot(activated_low, w_down, preferred_element_type=jnp.float32)
    ).astype(jnp.bfloat16)
    recon_own = jnp.dot(final_rows, w_head, preferred_element_type=jnp.float32).astype(jnp.bfloat16)
    reconstruction = lax.all_to_all(recon_own, "var", split_axis=1, concat_axis=0, tiled=True)
    cot_rows = lax.all_to_all(cotangent[0], "var", split_axis=0, concat_axis=1, tiled=True)
    final_grad = dot_last(cot_rows, w_head)
    head_grad = dot_first(final_rows, cot_rows)
    down_in = final_grad.astype(jnp.bfloat16)
    down_grad = dot_first(activated_low, down_in)
    act_grad = dot_last(down_in, w_down)
    (hidden_grad,) = gelu_pull(act_grad)
    hidden_low = hidden_grad.astype(jnp.bfloat16)
    up_grad = dot_first(normed_two, hidden_low)
    norm_two_grad = dot_last(hidden_low, w_up)
    middle_part, second_gain_grad, second_bias_grad = second_pull(norm_two_grad)
    middle_grad = final_grad + middle_part
    branch_in = middle_grad.astype(jnp.bfloat16)
    out_grad = dot_first(attention_output, branch_in)
    attended_grad = dot_last(branch_in, w_out).astype(jnp.bfloat16)
    qkv_grad = attention_backward(qkv_rows, allowed, log_total, attended_grad)
    qkv_weight_grad = dot_first(normed, qkv_grad)
    norm_grad = dot_last(qkv_grad, w_qkv)
    start_part, first_gain_grad, first_bias_grad = first_pull(norm_grad)
    start_grad = (middle_grad + start_part).astype(jnp.bfloat16)
    gathered = lax.all_gather(start_grad, "var", axis=0, tiled=True)
    pixel_grad = dot_last(gathered, w_embed).astype(jnp.bfloat16)
    embed_weight = dot_first(pixel_rows, gathered)
    w_embed_grad = lax.psum(embed_weight, "tok")
    shards = (
        lax.psum_scatter(qkv_weight_grad, "tok", scatter_dimension=0, tiled=True),
        lax.psum_scatter(out_grad, "tok", scatter_dimension=0, tiled=True),
        lax.psum_scatter(up_grad, "tok", scatter_dimension=0, tiled=True),
        lax.psum_scatter(down_grad, "tok", scatter_dimension=0, tiled=True),
        lax.psum_scatter(head_grad, "tok", scatter_dimension=0, tiled=True),
        lax.psum_scatter(first_gain_grad, "tok", scatter_dimension=0, tiled=True),
        lax.psum_scatter(first_bias_grad, "tok", scatter_dimension=0, tiled=True),
        lax.psum_scatter(second_gain_grad, "tok", scatter_dimension=0, tiled=True),
        lax.psum_scatter(second_bias_grad, "tok", scatter_dimension=0, tiled=True),
    )
    summed = (
        lax.psum(shards[0].astype(jnp.bfloat16), "var").astype(jnp.float32),
        lax.psum(shards[1].astype(jnp.bfloat16), "var").astype(jnp.float32),
        lax.psum(shards[2].astype(jnp.bfloat16), "var").astype(jnp.float32),
        lax.psum(shards[3].astype(jnp.bfloat16), "var").astype(jnp.float32),
        lax.psum(shards[4].astype(jnp.bfloat16), "var").astype(jnp.float32),
        lax.psum(shards[5].astype(jnp.bfloat16), "var").astype(jnp.float32),
        lax.psum(shards[6].astype(jnp.bfloat16), "var").astype(jnp.float32),
        lax.psum(shards[7].astype(jnp.bfloat16), "var").astype(jnp.float32),
        lax.psum(shards[8].astype(jnp.bfloat16), "var").astype(jnp.float32),
    )
    return (
        reconstruction[None],
        pixel_grad[None],
        w_embed_grad,
        summed[0],
        summed[1],
        summed[2],
        summed[3],
        summed[4],
        summed[5],
        summed[6],
        summed[7],
        summed[8],
    )


def solution(mesh):
    in_specs = (
        P("tok", None, "var"),
        P("var", None),
        P(),
        P(),
        P(),
        P(),
        P(),
        P(),
        P(),
        P(),
        P(),
        P("tok", "var"),
        P("tok", "var"),
        P("tok", "var"),
        P("tok", None, "var"),
    )
    out_specs = (
        P("tok", None, "var"),
        P("tok", None, "var"),
        P("var", None),
        P("tok", None),
        P("tok", None),
        P("tok", None),
        P("tok", None),
        P("tok", None),
        P("tok"),
        P("tok"),
        P("tok"),
        P("tok"),
    )
    return jax.shard_map(
        per_device, mesh=mesh, in_specs=in_specs, out_specs=out_specs, check_vma=False
    )
```

profile of v0, /device:TPU:0, one launch (start us, length us, event | category | flops | bytes accessed | tf_op | source)
XLA Modules:
  0.0 888.9 jit_solution(8028021262625007664)
XLA Ops:
  24.2 9.0 %multiply_sine_fusion.1 = (f32[1024,192]{1,0:T(8,128)}, f32[1024,192]{1,0:T(8,128)}, f32[1024,192]{1,0:T(8,128)}, f32[1024,192]{1,0:T(8,128)}) fusion(f32[192]{0:T(256)S(1)} %multiply_exponential_fusion, f32[1024]{0:T(1024)S(1)} %get-tuple-element.46, f32[1024]{0:T(1024)S(1)} %get-tuple-element.47), kind=kLoop, calls=%fused_computation.61 | loop fusion | flops 393216 | bytes 3154688 | tf_op jit(solution)/shard_map/sin | solution.py:31
  43.2 21.3 %reduce-scatter.7.cloned.1.call-done = bf16[1024,768]{1,0:T(8,128)(2,1)} async-done(((bf16[2048,768]{1,0:T(8,128)(2,1)}), bf16[1024,768]{1,0:T(8,128)(2,1)}) %reduce-scatter.7.cloned.1.call-update) | async-done | bytes 1572880 | tf_op jit(solution)/shard_map/reduce_scatter | solution.py:134
  96.7 10.4 %fusion.12 = (f32[2,12,512]{2,1,0:T(8,128)S(1)}, f32[2,12,512,512]{2,3,1,0:T(8,128)}) fusion(pred[2,512,512]{1,2,0:T(8,128)(4,1)S(1)} %copy-done.12, bf16[2,512,1,12,64]{1,0,4,3,2:T(2,128)(2,1)S(1)} %get-tuple-element.41, bf16[2,512,1,12,64]{1,0,4,3,2:T(2,128)(2,1)S(1)} %get-tuple-element.40), kind=kOutput, calls=%fused_computation.28 | convolution fusion | flops 824168448 | bytes 28884992 | tf_op jit(solution)/shard_map/snhd,smhd->shnm/dot_general | solution.py:63
  107.1 11.0 %fusion = f32[2,12,512]{2,1,0:T(8,128)S(1)} fusion(f32[2,12,512]{2,1,0:T(8,128)S(1)} %get-tuple-element.50, f32[2,12,512,512]{2,3,1,0:T(8,128)} %get-tuple-element.51, pred[2,512,512]{1,2,0:T(8,128)(4,1)S(1)} %copy-done.12), kind=kLoop, calls=%fused_computation.6 | loop fusion | flops 25153536 | bytes 25788416 | tf_op jit(solution)/shard_map/reduce_sum | solution.py:74
  118.8 11.9 %fusion.23 = bf16[2,512,12,64]{1,3,2,0:T(8,128)(2,1)S(1)} fusion(f32[2,12,512]{2,1,0:T(8,128)S(1)} %fusion, f32[2,12,512]{2,1,0:T(8,128)S(1)} %get-tuple-element.50, f32[2,12,512,512]{2,3,1,0:T(8,128)} %get-tuple-element.51, pred[2,512,512]{1,2,0:T(8,128)(4,1)S(1)} %copy-done.12, bf16[2,512,1,12,64]{1,0,4,3,2:T(2,128)(2,1)S(1)} %get-tuple-element.39), kind=kOutput, calls=%fused_computation.65 | convolution fusion | flops 837550080 | bytes 28934144 | tf_op jit(solution)/shard_map/shnm,smhd->snhd/dot_general | solution.py:76
  135.5 34.7 %multiply_convert_fusion.1 = (bf16[1024,3072]{1,0:T(8,128)(2,1)}, f32[1024,3072]{1,0:T(8,128)}, f32[1024,3072]{1,0:T(8,128)}) fusion(bf16[768,3072]{1,0:T(8,128)(2,1)S(1)} %bitcast.103, f32[1024,768]{1,0:T(8,128)S(1)} %get-tuple-element.53, f32[768]{0:T(1024)S(1)} %copy-done.21, f32[768]{0:T(1024)S(1)} %copy-done.20, f32[1024]{0:T(1024)S(1)} %fusion.40, ...), kind=kOutput, calls=%fused_computation.13 | convolution fusion | flops 5040242688 | bytes 39335936 | tf_op jit(solution)/shard_map/dot_general | solution.py:149
  170.2 18.3 %add_convert_fusion = bf16[1024,3072]{1,0:T(8,128)(2,1)} fusion(f32[1024,3072]{1,0:T(8,128)} %get-tuple-element.36, f32[1024,3072]{1,0:T(8,128)} %get-tuple-element.54, bf16[3072,768]{1,0:T(8,128)(2,1)} %param.20, f32[1024,768]{1,0:T(8,128)} %fusion.55), kind=kOutput, calls=%fused_computation.12 | convolution fusion | flops 4876664832 | bytes 39321600 | tf_op jit(solution)/shard_map/dot_general | solution.py:36
  188.5 10.4 %multiply_reduce_fusion.1 = (f32[768]{0:T(1024)}, f32[1024]{0:T(1024)S(1)}, f32[768]{0:T(1024)}, f32[1024,768]{1,0:T(8,128)S(1)}) fusion(f32[1024,768]{1,0:T(8,128)} %copy-done.1, f32[1024]{0:T(1024)S(1)} %fusion.40, f32[1024]{0:T(1024)S(1)} %broadcast_multiply_fusion, f32[768]{0:T(1024)S(1)} %copy-done.20, bf16[1024,3072]{1,0:T(8,128)(2,1)} %add_convert_fusion, ...), kind=kOutput, calls=%fused_computation.35 | convolution fusion | flops 4838126592 | bytes 17323008 | tf_op jit(solution)/shard_map/dot_general | solution.py:36
  217.3 19.0 %multiply_reduce_fusion = (f32[2,12,512]{2,1,0:T(8,128)}, f32[2,12,512,512]{2,3,1,0:T(8,128)}) fusion(f32[2,12,512]{2,1,0:T(8,128)} %log_add_fusion, f32[2,12,512,512]{2,3,1,0:T(8,128)} %get-tuple-element.51, pred[2,512,512]{1,2,0:T(8,128)(4,1)} %or_and_fusion, bf16[2,512,1,12,64]{1,0,4,3,2:T(2,128)(2,1)} %copy-done.16, bf16[2,512,12,64]{1,0,3,2:T(2,128)(2,1)} %reshape.195), kind=kOutput, calls=%fused_computation.1 | convolution fusion | flops 836751360 | bytes 54099968 | tf_op jit(solution)/shard_map/snhd,smhd->shnm/dot_general | solution.py:97
  236.3 22.1 %multiply_convert_fusion = bf16[2,12,512,512]{2,3,1,0:T(8,128)(2,1)} fusion(f32[2,12,512,512]{2,3,1,0:T(8,128)} %get-tuple-element.57, f32[2,12,512]{2,1,0:T(8,128)} %get-tuple-element.56, f32[2,12,512]{2,1,0:T(8,128)} %log_add_fusion, f32[2,12,512,512]{2,3,1,0:T(8,128)} %get-tuple-element.51, pred[2,512,512]{1,2,0:T(8,128)(4,1)} %or_and_fusion), kind=kLoop, calls=%fused_computation | loop fusion | flops 37748736 | bytes 63537152 | tf_op jit(solution)/shard_map/convert_element_type | solution.py:101
  258.4 9.9 %fusion.22 = bf16[2,512,1,12,64]{1,4,3,0,2:T(8,128)(2,1)} fusion(bf16[2,12,512,512]{2,3,1,0:T(8,128)(2,1)} %multiply_convert_fusion, bf16[2,512,1,12,64]{1,0,4,3,2:T(2,128)(2,1)S(1)} %copy-done.11), kind=kOutput, calls=%fused_computation.64 | convolution fusion | flops 806879232 | bytes 15728640 | tf_op jit(solution)/shard_map/shnm,snhd->smhd/dot_general | solution.py:105
  275.2 12.9 %fusion.18 = bf16[2,512,1,12,64]{1,4,3,0,2:T(8,128)(2,1)} fusion(f32[2,12,512]{2,1,0:T(8,128)S(1)} %copy-done.19, f32[2,12,512,512]{2,3,1,0:T(8,128)} %get-tuple-element.51, pred[2,512,512]{1,2,0:T(8,128)(4,1)S(1)} %copy-done.13, bf16[2,512,12,64]{1,0,3,2:T(2,128)(2,1)S(1)} %copy-done.17), kind=kOutput, calls=%fused_computation.62 | convolution fusion | flops 831258624 | bytes 28884992 | tf_op jit(solution)/shard_map/shnm,snhd->smhd/dot_general | solution.py:91
  291.9 9.4 %copy.84 = bf16[2,512,3,12,64]{1,0,4,3,2:T(2,128)(2,1)} copy(bf16[2,512,3,12,64]{1,4,3,0,2:T(8,128)(2,1)} %pad_maximum_fusion) | data formatting | bytes 9437184 | tf_op jit(solution)/shard_map/stack | solution.py:108
  314.8 10.4 %fusion.31 = f32[3072,768]{1,0:T(8,128)} fusion(bf16[1024,3072]{1,0:T(8,128)(2,1)} %get-tuple-element.35, f32[1024,768]{1,0:T(8,128)} %fusion.55), kind=kOutput, calls=%fused_computation.76 | convolution fusion | flops 4832624640 | bytes 18874368 | tf_op jit(solution)/shard_map/dot_general | solution.py:42
  325.3 11.6 %fusion.47 = f32[768,3072]{1,0:T(8,128)} fusion(bf16[1024,3072]{1,0:T(8,128)(2,1)} %add_convert_fusion, f32[1024,768]{1,0:T(8,128)} %copy-done.1, f32[768]{0:T(1024)S(1)} %copy-done.21, f32[768]{0:T(1024)S(1)} %copy-done.20, f32[1024]{0:T(1024)S(1)} %fusion.40, f32[1024]{0:T(1024)S(1)} %broadcast_multiply_fusion), kind=kOutput, calls=%fused_computation.113 | convolution fusion | flops 4835770368 | bytes 18888704 | tf_op jit(solution)/shard_map/dot_general | solution.py:42
  336.9 9.1 %add_convert_fusion.2 = bf16[1024,768]{1,0:T(8,128)(2,1)S(1)} fusion(f32[1024,768]{1,0:T(8,128)} %copy-done.1, bf16[1024,3072]{1,0:T(8,128)(2,1)} %get-tuple-element.35, bf16[3072,768]{1,0:T(8,128)(2,1)} %param.20), kind=kOutput, calls=%fused_computation.43 | convolution fusion | flops 4833411072 | bytes 15728640 | tf_op jit(solution)/shard_map/dot_general | solution.py:153
  364.9 40.8 %reduce-scatter.9.cloned.1.call-done = f32[48,2304]{1,0:T(8,128)} async-done(((f32[768,2304]{1,0:T(8,128)}), f32[48,2304]{1,0:T(8,128)}) %reduce-scatter.9.cloned.1.call-update) | async-done | bytes 442384 | tf_op jit(solution)/shard_map/reduce_scatter | solution.py:182
  407.4 113.7 %reduce-scatter.15.cloned.1.call-done = f32[192,768]{1,0:T(8,128)} async-done(((f32[3072,768]{1,0:T(8,128)}), f32[192,768]{1,0:T(8,128)}) %reduce-scatter.15.cloned.1.call-update) | async-done | bytes 589840 | tf_op jit(solution)/shard_map/reduce_scatter | solution.py:185
  522.9 113.3 %reduce-scatter.13.cloned.1.call-done = f32[48,3072]{1,0:T(8,128)} async-done(((f32[768,3072]{1,0:T(8,128)}), f32[48,3072]{1,0:T(8,128)}) %reduce-scatter.13.cloned.1.call-update) | async-done | bytes 589840 | tf_op jit(solution)/shard_map/reduce_scatter | solution.py:184
  647.4 60.3 %all-reduce.4 = (bf16[768]{0:T(1024)(128)(2,1)}, bf16[768]{0:T(1024)(128)(2,1)}, bf16[768]{0:T(1024)(128)(2,1)}, bf16[768]{0:T(1024)(128)(2,1)}) all-reduce(f32[768]{0:T(1024)S(1)} %copy-done.37, f32[768]{0:T(1024)S(1)} %copy-done.38, f32[768]{0:T(1024)S(1)} %copy-done.35, ...), channel_id=8, replica_groups=mesh['var'=2,'tok'=16] {'tok'}, use_global_device_ids=true, to_apply=%region_24.25.clone | all-reduce | flops 3072 | bytes 18432
  717.7 10.7 %all-reduce.5 = (bf16[48,320]{1,0:T(8,128)(2,1)}, bf16[48]{0:T(256)(128)(2,1)}, bf16[48]{0:T(256)(128)(2,1)}, bf16[48]{0:T(256)(128)(2,1)}, bf16[48]{0:T(256)(128)(2,1)}) all-reduce(bf16[48,320]{1,0:T(8,128)(2,1)} %convert_element_type.173, bf16[48]{0:T(256)(128)(2,1)S(1)} %dynamic-slice.15, ...), channel_id=1, replica_groups=mesh['var'=2,'tok'=16] {'var'}, use_global_device_ids=true, to_apply=%region_22.23 | all-reduce | flops 15552 | bytes 62208 | tf_op jit(solution)/shard_map/psum | solution.py:197
  734.4 10.2 %all-gather.2.cloned.1.call-done = bf16[2048,768]{1,0:T(8,128)(2,1)} async-done(((bf16[1024,768]{1,0:T(8,128)(2,1)}), bf16[2048,768]{1,0:T(8,128)(2,1)}) %all-gather.2.cloned.1.call-update) | async-done | bytes 3145744 | tf_op jit(solution)/shard_map/all_gather | solution.py:177
  752.1 32.8 %all-reduce.12.cloned.1.call-done = (bf16[48,2304]{1,0:T(8,128)(2,1)}, bf16[48,768]{1,0:T(8,128)(2,1)}, bf16[48,3072]{1,0:T(8,128)(2,1)}, bf16[192,768]{1,0:T(8,128)(2,1)}) async-done(((bf16[48,2304]{1,0:T(8,128)(2,1)}, bf16[48,768]{1,0:T(8,128)(2,1)}, bf16[48,3072]{1,0:T(8,128)(2,1)}, bf16[192,768]{1,0:T(8,128)(2,1)}), (bf16[48,2304]{1,0:T(8,128)(2,1)}, bf16[48,768]{1,0:T(8,128)(2,1)}, ...) | async-done | bytes 884752 | tf_op jit(solution)/shard_map/psum | solution.py:193
  791.8 88.5 %all-reduce.10.cloned.1.call-done = f32[160,768]{1,0:T(8,128)} async-done(((f32[160,768]{1,0:T(8,128)}), f32[160,768]{1,0:T(8,128)}) %all-reduce.10.cloned.1.call-update) | async-done | bytes 491536 | tf_op jit(solution)/shard_map/psum | solution.py:180
  (186 shorter events, 171.9 us)
Async XLA Ops:
  7.2 63.2 %copy-start = (bf16[768,2304]{1,0:T(8,128)(2,1)S(1)}, bf16[768,2304]{1,0:T(8,128)(2,1)}, u32[]{:S(2)}) copy-start(bf16[768,2304]{1,0:T(8,128)(2,1)} %param.17) | copy-start | bytes 10616836
  7.2 57.3 %reduce-scatter.7.cloned.1.call-start = ((), (), s32[]{:S(2)}) async-start(), calls=%async_computation.8 | async-start | bytes 4718592 | tf_op jit(solution)/shard_map/reduce_scatter | solution.py:134
  11.2 9.6 %copy-start.34 = (s32[1,1024]{1,0:T(1,128)S(1)}, s32[1,1024]{1,0:T(1,128)}, u32[]{:S(2)}) copy-start(s32[1,1024]{1,0:T(1,128)} %param.28) | copy-start | bytes 12292
  11.2 11.6 %copy-start.33 = (s32[1,1024]{1,0:T(1,128)S(1)}, s32[1,1024]{1,0:T(1,128)}, u32[]{:S(2)}) copy-start(s32[1,1024]{1,0:T(1,128)} %param.26) | copy-start | bytes 12292
  16.3 22.8 %all-to-all-start.1 = ((bf16[2,1024,160]{1,2,0:T(8,128)(2,1)}), bf16[2,1024,160]{1,2,0:T(8,128)(2,1)}, u32[]{:S(2)}, u32[]{:S(2)}) async-start(bf16[2,1024,160]{1,2,0:T(8,128)(2,1)} %copy.77), calls=%async_computation.2 | async-start | bytes 1310720 | tf_op jit(solution)/shard_map/all_to_all | solution.py:157
  20.6 342.8 %reduce-scatter.11.cloned.1.call-start = ((), (), s32[]{:S(2)}) async-start(), calls=%async_computation.12 | async-start | bytes 2506752 | tf_op jit(solution)/shard_map/reduce_scatter | solution.py:183
  96.7 10.4 %copy-start.8 = (bf16[2,512,1,12,64]{1,0,4,3,2:T(2,128)(2,1)}, bf16[2,512,1,12,64]{1,0,4,3,2:T(2,128)(2,1)S(1)}, u32[]{:S(2)}) copy-start(bf16[2,512,1,12,64]{1,0,4,3,2:T(2,128)(2,1)S(1)} %get-tuple-element.41) | copy-start | bytes 4718596
  96.7 10.4 %copy-start.10 = (bf16[2,512,1,12,64]{1,0,4,3,2:T(2,128)(2,1)}, bf16[2,512,1,12,64]{1,0,4,3,2:T(2,128)(2,1)S(1)}, u32[]{:S(2)}) copy-start(bf16[2,512,1,12,64]{1,0,4,3,2:T(2,128)(2,1)S(1)} %get-tuple-element.40) | copy-start | bytes 4718596
  96.7 22.1 %copy-start.16 = (bf16[2,512,1,12,64]{1,0,4,3,2:T(2,128)(2,1)}, bf16[2,512,1,12,64]{1,0,4,3,2:T(2,128)(2,1)S(1)}, u32[]{:S(2)}) copy-start(bf16[2,512,1,12,64]{1,0,4,3,2:T(2,128)(2,1)S(1)} %get-tuple-element.39) | copy-start | bytes 4718596
  134.6 35.6 %copy-start.1 = (f32[1024,768]{1,0:T(8,128)}, f32[1024,768]{1,0:T(8,128)S(1)}, u32[]{:S(2)}) copy-start(f32[1024,768]{1,0:T(8,128)S(1)} %get-tuple-element.53) | copy-start | bytes 9437188
  188.5 10.4 %copy-start.2 = (f32[1024,768]{1,0:T(8,128)S(1)}, f32[1024,768]{1,0:T(8,128)}, u32[]{:S(2)}) copy-start(f32[1024,768]{1,0:T(8,128)} %copy-done.1) | copy-start | bytes 9437188
  210.6 195.1 %reduce-scatter.9.cloned.1.call-start = ((), (), s32[]{:S(2)}) async-start(), calls=%async_computation.11 | async-start | bytes 7520256 | tf_op jit(solution)/shard_map/reduce_scatter | solution.py:182
  236.3 22.1 %copy-start.11 = (bf16[2,512,1,12,64]{1,0,4,3,2:T(2,128)(2,1)S(1)}, bf16[2,512,1,12,64]{1,0,4,3,2:T(2,128)(2,1)}, u32[]{:S(2)}) copy-start(bf16[2,512,1,12,64]{1,0,4,3,2:T(2,128)(2,1)} %copy-done.10) | copy-start | bytes 4718596
  258.4 9.9 %copy-start.9 = (bf16[2,512,1,12,64]{1,0,4,3,2:T(2,128)(2,1)S(1)}, bf16[2,512,1,12,64]{1,0,4,3,2:T(2,128)(2,1)}, u32[]{:S(2)}) copy-start(bf16[2,512,1,12,64]{1,0,4,3,2:T(2,128)(2,1)} %copy-done.8) | copy-start | bytes 4718596
  314.7 206.4 %reduce-scatter.15.cloned.1.call-start = ((), (), s32[]{:S(2)}) async-start(), calls=%async_computation.14 | async-start | bytes 10027008 | tf_op jit(solution)/shard_map/reduce_scatter | solution.py:185
  325.2 311.0 %reduce-scatter.13.cloned.1.call-start = ((), (), s32[]{:S(2)}) async-start(), calls=%async_computation.13 | async-start | bytes 10027008 | tf_op jit(solution)/shard_map/reduce_scatter | solution.py:184
  336.9 379.3 %reduce-scatter.17.cloned.1.call-start = ((), (), s32[]{:S(2)}) async-start(), calls=%async_computation.15 | async-start | bytes 1253376 | tf_op jit(solution)/shard_map/reduce_scatter | solution.py:186
  350.5 394.1 %all-gather.2.cloned.1.call-start = ((), (), s32[]{:S(2)}) async-start(), calls=%async_computation.9 | async-start | bytes 4718592 | tf_op jit(solution)/shard_map/all_gather | solution.py:177
  363.3 421.6 %all-reduce.12.cloned.1.call-start = ((), (), s32[]{:S(2)}) async-start(), calls=%async_computation.16 | async-start | bytes 1769472 | tf_op jit(solution)/shard_map/psum | solution.py:193
  638.1 9.3 %copy-start.35 = (f32[768]{0:T(1024)S(1)}, f32[768]{0:T(1024)}, u32[]{:S(2)}) copy-start(f32[768]{0:T(1024)} %get-tuple-element.12) | copy-start | bytes 9220
  638.1 9.3 %copy-start.36 = (f32[768]{0:T(1024)S(1)}, f32[768]{0:T(1024)}, u32[]{:S(2)}) copy-start(f32[768]{0:T(1024)} %get-tuple-element.16) | copy-start | bytes 9220
  638.1 9.3 %copy-start.37 = (f32[768]{0:T(1024)S(1)}, f32[768]{0:T(1024)}, u32[]{:S(2)}) copy-start(f32[768]{0:T(1024)} %get-tuple-element.14) | copy-start | bytes 9220
  641.2 69.5 %all-to-all-start = ((bf16[1024,2,160]{0,2,1:T(8,128)(2,1)}), bf16[1024,2,160]{0,2,1:T(8,128)(2,1)}, u32[]{:S(2)}, u32[]{:S(2)}) async-start(bf16[1024,2,160]{0,2,1:T(8,128)(2,1)} %bitcast.100), calls=%async_computation.1 | async-start | bytes 1310720 | tf_op jit(solution)/shard_map/all_to_all | solution.py:156
  645.4 234.9 %all-reduce.10.cloned.1.call-start = ((), (), s32[]{:S(2)}) async-start(), calls=%async_computation.10 | async-start | bytes 983040 | tf_op jit(solution)/shard_map/psum | solution.py:180
  (32 other events, 123.6 us)
Sparse Core Ops, SparseCore 0:
  11.4 53.0 reduce-scatter.6
  210.7 62.9 reduce-scatter.10
  314.8 90.8 reduce-scatter.8
  410.2 110.8 reduce-scatter.14
  525.1 111.1 reduce-scatter.12
  640.1 57.9 reduce-scatter.16
  699.7 44.8 all-gather.1
  747.8 36.9 all-reduce.11
  789.2 91.0 all-reduce.9
where the time goes:
time: 893 us; the launch traced here: 889 us
  waiting for transfers between devices  427 us (48%)
  matrix products  218 us (24%)
  other arithmetic  80.4 us (9%)
  blocking collectives  71 us (8%)
  local copies, waits for them, and re-layouts  67.9 us (8%)
  between operations  15.3 us (2%)
  starting transfers between devices  9.24 us (1%)
    reduce_scatter x1, waiting for transfers between devices, per_device(): lax.psum_scatter(down_grad, 'tok', scatter_dimension=0, tiled=True)  114 us
    reduce_scatter x1, waiting for transfers between devices, per_device(): lax.psum_scatter(up_grad, 'tok', scatter_dimension=0, tiled=True)  113 us
    psum x1, waiting for transfers between devices, per_device(): w_embed_grad = lax.psum(embed_weight, 'tok')  88.5 us
    unnamed x1, blocking collectives  60.3 us
    dot_general x6, matrix products, dot_last(): lax.dot_general(left, right, (((1,), (1,)), ((), ())), preferred_element_...  50.3 us
    reduce_scatter x1, waiting for transfers between devices, per_device(): lax.psum_scatter(qkv_weight_grad, 'tok', scatter_dimension=0, tiled=True)  40.8 us
    dot_general x6, matrix products, dot_first(): lax.dot_general(left, right, (((0,), (0,)), ((), ())), preferred_element_...  38.7 us
    dot_general x1, matrix products, per_device(): hidden = jnp.dot(normed_two, w_up, preferred_element_type=jnp.float32)  34.7 us
  transfers between devices with their start and end apart: 11, of which 8 were waited for; matrix products, arithmetic and copies ran while one was open for 23% of the time, Pallas kernels for 0%

commit v1 on v0

v1 whole, which is shorter than its diff:
```python
import functools
import math

import jax
import jax.numpy as jnp
from jax import lax
from jax.experimental import pallas as pl
from jax.experimental.pallas import tpu as pltpu
from jax.sharding import PartitionSpec as P

HEADS = 12
HEAD_SIZE = 64
BIG = 512
BIG_COLS = 32
D = 768
FF = 3072
TILE = 256
SHARDS = 16
ROWS = D // SHARDS
EMBED_ROWS = 192
MESH = pl.DeviceIdType.MESH
F32 = jnp.float32
BF16 = jnp.bfloat16
VMEM_LIMIT = 60 * 2**20


def nn(left, right):
    return lax.dot_general(left, right, (((1,), (0,)), ((), ())), preferred_element_type=F32)


def nt(left, right):
    return lax.dot_general(left, right, (((1,), (1,)), ((), ())), preferred_element_type=F32)


def tn(left, right):
    return lax.dot_general(left, right, (((0,), (0,)), ((), ())), preferred_element_type=F32)


def whole():
    return pl.BlockSpec(memory_space=pltpu.VMEM)


def params(**more):
    return pltpu.CompilerParams(vmem_limit_bytes=VMEM_LIMIT, **more)


def shape(dims, dtype):
    return jax.ShapeDtypeStruct(dims, dtype)


def norm_stats(rows):
    center = rows - jnp.mean(rows, axis=-1, keepdims=True)
    rstd = lax.rsqrt(jnp.mean(center * center, axis=-1, keepdims=True) + 1e-06)
    return center * rstd, rstd


def norm_backward(upstream, unit, rstd, gain):
    scaled = upstream * gain
    first = jnp.mean(scaled, axis=-1, keepdims=True)
    second = jnp.mean(scaled * unit, axis=-1, keepdims=True)
    return rstd * (scaled - first - unit * second)


def place_tables(high_ref, low_ref):
    lane = lax.broadcasted_iota(jnp.int32, (64, D), 1)
    sub = lax.broadcasted_iota(jnp.int32, (64, D), 0)
    quarter = D // 4
    part = jnp.where(lane < quarter, 0, jnp.where(lane < 2 * quarter, 1, jnp.where(lane < 3 * quarter, 2, 3)))
    ladder = (lane - part * quarter).astype(F32) / quarter
    frequency = jnp.exp(-math.log(10000.0) * ladder)
    cell = jnp.where(sub < BIG_COLS, sub, sub - BIG_COLS).astype(F32)
    angle = cell * frequency
    wave = jnp.where((part == 0) | (part == 2), jnp.sin(angle), jnp.cos(angle))
    mine = jnp.where(sub < BIG_COLS, 1, 0) == jnp.where(part < 2, 1, 0)
    wave = jnp.where(mine, wave, 0.0)
    high = wave.astype(BF16)
    high_ref[...] = high
    low_ref[...] = (wave - high.astype(F32)).astype(BF16)


def first_kernel(pix_ref, cell_ref, emb_ref, wqkv_ref, gain_ref, bias_ref, start_ref, normed_ref, qkv_ref, high_ref, low_ref):
    @pl.when(pl.program_id(0) == 0)
    def _():
        place_tables(high_ref, low_ref)

    cells = cell_ref[...]
    sub = lax.broadcasted_iota(jnp.int32, (64, TILE), 0)
    row_of = lax.shift_right_logical(cells, 5)
    col_of = jnp.bitwise_and(cells, BIG_COLS - 1)
    wanted = jnp.where(sub < BIG_COLS, row_of, col_of + BIG_COLS)
    hot = jnp.where(sub == wanted, 1.0, 0.0).astype(BF16)
    start = nn(pix_ref[...], emb_ref[...]) + (tn(hot, high_ref[...]) + tn(hot, low_ref[...]))
    start_ref[...] = start
    unit, _ = norm_stats(start)
    normed = (unit * gain_ref[...] + bias_ref[...]).astype(BF16)
    normed_ref[...] = normed
    for part in range(3):
        cols = slice(part * D, (part + 1) * D)
        rows = nn(normed, wqkv_ref[:, cols])
        if part == 0:
            rows = rows * HEAD_SIZE ** (-0.5)
        qkv_ref[:, cols] = rows.astype(BF16)


def first_call(pix, cells, w_embed, w_qkv, gain, bias):
    rows = pix.shape[0]
    tile = lambda width: pl.BlockSpec((TILE, width), lambda i: (i, 0))
    return pl.pallas_call(
        first_kernel,
        grid=(rows // TILE,),
        in_specs=[tile(pix.shape[1]), pl.BlockSpec((1, TILE), lambda i: (0, i)), whole(), whole(), whole(), whole()],
        out_specs=[tile(D), tile(D), tile(3 * D)],
        out_shape=[shape((rows, D), F32), shape((rows, D), BF16), shape((rows, 3 * D), BF16)],
        scratch_shapes=[pltpu.VMEM((64, D), BF16), pltpu.VMEM((64, D), BF16)],
        compiler_params=params(),
        name="first",
    )(pix, cells, w_embed, w_qkv, gain, bias)


def attend_kernel(q_ref, k_ref, v_ref, id_ref, seen_ref, out_ref, prob_ref, mask_ref):
    @pl.when(pl.program_id(1) == 0)
    def _():
        ids = id_ref[...].astype(F32)
        seen = seen_ref[...].astype(F32)
        code = jnp.broadcast_to(ids * 2.0 + jnp.where(seen == 1.0, 1.0, 0.0), (128, BIG))
        column = jnp.transpose(code)[:, :1]
        key_id = jnp.floor(column * 0.5)
        key_seen = column - 2.0 * key_id
        row = lax.broadcasted_iota(jnp.int32, (BIG, BIG), 0)
        col = lax.broadcasted_iota(jnp.int32, (BIG, BIG), 1)
        allowed = (key_id == ids) & ((key_seen == 1.0) | (row == col))
        mask_ref[...] = jnp.where(allowed, 0.0, -1e30)

    lane = lax.broadcasted_iota(jnp.int32, (BIG, 128), 1)
    keys = k_ref[...]
    flipped = jnp.transpose(v_ref[...])
    outs = []
    for head in range(2):
        mine = (lane < HEAD_SIZE) if head == 0 else (lane >= HEAD_SIZE)
        scores = nt(jnp.where(mine, keys, jnp.zeros_like(keys)), q_ref[...]) + mask_ref[...]
        lifted = jnp.exp(scores - jnp.max(scores, axis=0, keepdims=True))
        prob = (lifted * (1.0 / jnp.sum(lifted, axis=0, keepdims=True))).astype(BF16)
        prob_ref[head] = prob
        outs.append(nn(flipped[head * HEAD_SIZE : (head + 1) * HEAD_SIZE], prob))
    out_ref[...] = jnp.transpose(jnp.concatenate(outs, axis=0)).astype(BF16)


def attend_call(qkv, ids, seen):
    rows = qkv.shape[0]
    pairs = HEADS // 2
    block = lambda off: pl.BlockSpec((BIG, 128), lambda s, h: (s, h + off))
    line = pl.BlockSpec((1, BIG), lambda s, h: (0, s))
    return pl.pallas_call(
        attend_kernel,
        grid=(rows // BIG, pairs),
        in_specs=[block(0), block(pairs), block(2 * pairs), line, line],
        out_specs=[block(0), pl.BlockSpec((2, BIG, BIG), lambda s, h: (s * pairs + h, 0, 0))],
        out_shape=[shape((rows, D), BF16), shape((rows // BIG * HEADS, BIG, BIG), BF16)],
        scratch_shapes=[pltpu.VMEM((BIG, BIG), F32)],
        compiler_params=params(),
        name="attend",
    )(qkv, qkv, qkv, ids, seen)


def gelu_pair(hidden):
    power = jnp.exp(hidden * hidden * -0.5)
    cdf = 0.5 + 0.5 * lax.erf(hidden * math.sqrt(0.5))
    return hidden * cdf, cdf + hidden * power * (1.0 / math.sqrt(2.0 * math.pi))


def middle_kernel(
    att_ref, start_ref, cot_ref, wout_ref, wup_ref, wdown_ref, whead_ref, gain_ref, bias_ref,
    recon_ref, act_ref, n2_ref, hid_ref, final_ref, downin_ref, branch_ref, mid_ref, attg_ref, gains_ref, slope_ref,
):
    middle = start_ref[...] + nn(att_ref[...], wout_ref[...])
    unit, rstd = norm_stats(middle)
    n2 = (unit * gain_ref[...] + bias_ref[...]).astype(BF16)
    n2_ref[...] = n2
    for j in range(FF // D):
        cols = slice(j * D, (j + 1) * D)
        act, slope = gelu_pair(nn(n2, wup_ref[:, cols]))
        act_ref[:, cols] = act.astype(BF16)
        slope_ref[:, cols] = slope
    final = (middle + nn(act_ref[...], wdown_ref[...])).astype(BF16)
    final_ref[...] = final
    recon_ref[...] = nn(final, whead_ref[...]).astype(BF16)
    final_grad = nt(cot_ref[...], whead_ref[...])
    down_in = final_grad.astype(BF16)
    downin_ref[...] = down_in
    for j in range(FF // D):
        cols = slice(j * D, (j + 1) * D)
        hid_ref[:, cols] = (nt(down_in, wdown_ref[cols, :]) * slope_ref[:, cols]).astype(BF16)
    upstream = nt(hid_ref[...], wup_ref[...])
    gains = jnp.concatenate(
        [jnp.sum(upstream * unit, axis=0, keepdims=True), jnp.sum(upstream, axis=0, keepdims=True), jnp.zeros((6, D), F32)], axis=0
    )

    @pl.when(pl.program_id(0) == 0)
    def _():
        gains_ref[...] = gains

    @pl.when(pl.program_id(0) > 0)
    def _():
        gains_ref[...] += gains

    mid = final_grad + norm_backward(upstream, unit, rstd, gain_ref[...])
    mid_ref[...] = mid
    branch = mid.astype(BF16)
    branch_ref[...] = branch
    attg_ref[...] = nt(branch, wout_ref[...]).astype(BF16)


def middle_call(att, start, cot, w_out, w_up, w_down, w_head, gain, bias):
    rows = att.shape[0]
    wide = cot.shape[1]
    tile = lambda width: pl.BlockSpec((TILE, width), lambda i: (i, 0))
    widths = [(wide, BF16), (FF, BF16), (D, BF16), (FF, BF16), (D, BF16), (D, BF16), (D, BF16), (D, F32), (D, BF16)]
    return pl.pallas_call(
        middle_kernel,
        grid=(rows // TILE,),
        in_specs=[tile(D), tile(D), tile(wide)] + [whole()] * 6,
        out_specs=[tile(w) for w, _ in widths] + [pl.BlockSpec((8, D), lambda i: (0, 0))],
        out_shape=[shape((rows, w), t) for w, t in widths] + [shape((8, D), F32)],
        scratch_shapes=[pltpu.VMEM((TILE, FF), F32)],
        compiler_params=params(),
        name="middle",
    )(att, start, cot, w_out, w_up, w_down, w_head, gain, bias)


def attend_back_kernel(q_ref, k_ref, v_ref, att_ref, attg_ref, prob_ref, dq_ref, dk_ref, dv_ref):
    lane = lax.broadcasted_iota(jnp.int32, (BIG, 128), 1)
    grad = attg_ref[...]
    values = v_ref[...]
    query = q_ref[...]
    flat = jnp.transpose(att_ref[...].astype(F32) * grad.astype(F32))
    keys = jnp.transpose(k_ref[...])
    dq, dk, dv = [], [], []
    for head in range(2):
        span = slice(head * HEAD_SIZE, (head + 1) * HEAD_SIZE)
        mine = (lane < HEAD_SIZE) if head == 0 else (lane >= HEAD_SIZE)
        prob = prob_ref[head]
        prob_grad = nt(jnp.where(mine, values, jnp.zeros_like(values)), grad)
        row_dot = jnp.sum(flat[span], axis=0, keepdims=True)
        score_grad = (prob.astype(F32) * (prob_grad - row_dot)).astype(BF16)
        dv.append(nn(prob, grad))
        dk.append(nn(score_grad, query))
        dq.append(nn(keys[span], score_grad))
    low = lane < HEAD_SIZE
    dv_ref[...] = jnp.where(low, dv[0], dv[1]).astype(BF16)
    dk_ref[...] = jnp.where(low, dk[0], dk[1]).astype(BF16)
    dq_ref[...] = (jnp.transpose(jnp.concatenate(dq, axis=0)) * HEAD_SIZE ** (-0.5)).astype(BF16)


def attend_back_call(qkv, att, attg, prob):
    rows = qkv.shape[0]
    pairs = HEADS // 2
    block = lambda off: pl.BlockSpec((BIG, 128), lambda s, h: (s, h + off))
    return pl.pallas_call(
        attend_back_kernel,
        grid=(rows // BIG, pairs),
        in_specs=[block(0), block(pairs), block(2 * pairs), block(0), block(0), pl.BlockSpec((2, BIG, BIG), lambda s, h: (s * pairs + h, 0, 0))],
        out_specs=[block(0)] * 3,
        out_shape=[shape((rows, D), BF16)] * 3,
        compiler_params=params(),
        name="attend_back",
    )(qkv, qkv, qkv, att, attg, prob)


def last_kernel(dq_ref, dk_ref, dv_ref, start_ref, mid_ref, wqkv_ref, emb_ref, gain_ref, sg_ref, pg_ref, gains_ref):
    upstream = nt(dq_ref[...], wqkv_ref[:, :D]) + nt(dk_ref[...], wqkv_ref[:, D : 2 * D]) + nt(dv_ref[...], wqkv_ref[:, 2 * D :])
    unit, rstd = norm_stats(start_ref[...])
    gains = jnp.concatenate(
        [jnp.sum(upstream * unit, axis=0, keepdims=True), jnp.sum(upstream, axis=0, keepdims=True), jnp.zeros((6, D), F32)], axis=0
    )

    @pl.when(pl.program_id(0) == 0)
    def _():
        gains_ref[...] = gains

    @pl.when(pl.program_id(0) > 0)
    def _():
        gains_ref[...] += gains

    start_grad = (mid_ref[...] + norm_backward(upstream, unit, rstd, gain_ref[...])).astype(BF16)
    sg_ref[...] = start_grad
    pg_ref[...] = nt(start_grad, emb_ref[...]).astype(BF16)


def last_call(dq, dk, dv, start, mid, w_qkv, w_embed, gain):
    rows = dq.shape[0]
    tile = lambda width: pl.BlockSpec((TILE, width), lambda i: (i, 0))
    wide = w_embed.shape[0]
    return pl.pallas_call(
        last_kernel,
        grid=(rows // TILE,),
        in_specs=[tile(D)] * 5 + [whole()] * 3,
        out_specs=[tile(D), tile(wide), pl.BlockSpec((8, D), lambda i: (0, 0))],
        out_shape=[shape((rows, D), BF16), shape((rows, wide), BF16), shape((8, D), F32)],
        compiler_params=params(),
        name="last",
    )(dq, dk, dv, start, mid, w_qkv, w_embed, gain)


def weight_kernel(left_ref, right_ref, out_ref):
    out_ref[...] = tn(left_ref[...], right_ref[...]).astype(BF16)


def weight_call(left, right, name):
    rows, height = left.shape
    width = right.shape[1]
    high = min(height, D)
    wide = min(width, D)
    return pl.pallas_call(
        weight_kernel,
        grid=(height // high, width // wide),
        in_specs=[pl.BlockSpec((rows, high), lambda i, j: (0, i)), pl.BlockSpec((rows, wide), lambda i, j: (0, j))],
        out_specs=pl.BlockSpec((high, wide), lambda i, j: (i, j)),
        out_shape=shape((height, width), BF16),
        compiler_params=params(),
        name=name,
    )(left, right)


def bit_of(index, bit, low):
    return lax.rem(lax.div(index, low * 2**bit), 2)


def send_to(source, target, send, recv, device):
    copy = pltpu.make_async_remote_copy(
        src_ref=source, dst_ref=target, send_sem=send, recv_sem=recv, device_id=device, device_id_type=MESH
    )
    copy.start()
    return copy


def place(keep, cols):
    return tuple(keep[b] if b in keep else slice(None) for b in (3, 2, 1, 0)) + (slice(None), cols)


def halves(order):
    return order[-1] != "x"


def unit_scratch(order, wide):
    free, out = 4, []
    for axis in order:
        if axis != "x":
            free -= 1
        elif halves(order):
            wide = wide // 2
        out.append(pltpu.VMEM((2,) * free + (ROWS, wide), BF16))
    if halves(order):
        out.append(pltpu.VMEM((ROWS, wide), BF16))
    return out + [pltpu.SemaphoreType.DMA((len(out),)), pltpu.SemaphoreType.DMA((len(out),))]


def unit_job(grad, write, order, wide, partner, bits_of, pool):
    count = len(order) + halves(order)
    bufs = [pool.pop(0) for _ in range(count)]
    send, recv = pool.pop(0), pool.pop(0)
    keep, cols = {}, slice(None)
    half = wide // 2
    span = lambda bit: pl.ds(pl.multiple_of(bit * half, half), half)
    for step, axis in enumerate(order):
        mine = bits_of[axis]
        other, sent = dict(keep), cols
        if axis != "x":
            other[axis] = 1 - mine
            keep = {**keep, axis: mine}
        elif halves(order):
            cols, sent = span(mine), span(1 - mine)
        copy = send_to(grad.at[place(other, sent)], bufs[step], send.at[step], recv.at[step], partner[axis])
        yield True
        copy.wait()
        here = place(keep, cols)
        total = grad[here].astype(F32) + bufs[step][...].astype(F32)
        if step < count - 1:
            grad[here] = total.astype(BF16)
        else:
            write(slice(None), total)
    if halves(order):
        step = len(order)
        copy = send_to(grad.at[here], bufs[step], send.at[step], recv.at[step], partner["x"])
        yield True
        copy.wait()
        write(span(bits_of["x"]), grad[here].astype(F32))
        write(span(1 - bits_of["x"]), bufs[step][...].astype(F32))


def embed_scratch():
    half, rows = D // 2, EMBED_ROWS
    sizes = [(rows, D), (rows, half)] + [(rows // 2, half)] * 4 + [(rows, half)]
    return [pltpu.VMEM(size, BF16) for size in sizes] + [pltpu.SemaphoreType.DMA((7,)), pltpu.SemaphoreType.DMA((7,))]


def embed_job(grad, write, partner, bits_of, pool):
    bufs = [pool.pop(0) for _ in range(7)]
    send, recv = pool.pop(0), pool.pop(0)
    var = bits_of["x"]
    half, rows = D // 2, EMBED_ROWS // 2
    own = grad.at[var]
    every = slice(None)
    pick = lambda bit: pl.ds(pl.multiple_of(bit * half, half), half)
    line = lambda bit: pl.ds(pl.multiple_of(bit * rows, rows), rows)
    core, side = bits_of[0], bits_of[1]
    here = (line(side), pick(core))
    plan = [
        ("x", None, (every, every)),
        (0, (every, pick(1 - core)), (every, pick(core))),
        (1, (line(1 - side), pick(core)), here),
        (2, here, here),
        (3, here, here),
    ]
    for step, (axis, out, keep) in enumerate(plan):
        source = grad.at[1 - var] if out is None else own.at[out]
        copy = send_to(source, bufs[step], send.at[step], recv.at[step], partner[axis])
        yield True
        copy.wait()
        own[keep] = (own[keep].astype(F32) + bufs[step][...].astype(F32)).astype(BF16)
    copy = send_to(own.at[here], bufs[5], send.at[5], recv.at[5], partner[1])
    yield True
    copy.wait()
    own[line(1 - side), pick(core)] = bufs[5][...]
    copy = send_to(own.at[every, pick(core)], bufs[6], send.at[6], recv.at[6], partner[0])
    yield True
    copy.wait()
    write(pick(core), own[every, pick(core)].astype(F32))
    write(pick(1 - core), bufs[6][...].astype(F32))


ORDER_A = (0, "x", 1, 2, 3)
ORDER_B = (0, 1, 2, 3, "x")
ORDER_C = (0, 2, 3, 1, "x")
NARROW = 384
UNITS = (
    ("down", 0, ORDER_A),
    ("down", 1, ORDER_B),
    ("down", 2, ORDER_A),
    ("down", 3, ORDER_B),
    ("up", 0, ORDER_A),
    ("up", 1, ORDER_B),
    ("up", 2, ORDER_A),
    ("up", 3, ORDER_C),
    ("out", 0, ORDER_B),
    ("head", 0, ORDER_C),
    ("q", 0, ORDER_A),
    ("k", 0, ORDER_B),
    ("v", 0, ORDER_A),
)
NAMES = ("down", "up", "out", "head", "q", "k", "v")


def unit_wide(name):
    return NARROW if name == "head" else D


def meet(partner):
    barrier = pltpu.get_barrier_semaphore()
    for device in partner.values():
        pl.semaphore_signal(barrier, inc=1, device_id=device, device_id_type=MESH)
    pl.semaphore_wait(barrier, len(partner))


def neighbours(low):
    var, tok = lax.axis_index("var"), lax.axis_index("tok")
    bits_of = {b: bit_of(tok, b, low) for b in range(4)}
    partner = {b: (var, tok + low * 2**b * (1 - 2 * bits_of[b])) for b in range(4)}
    return {**partner, "x": (1 - var, tok)}, {**bits_of, "x": var}


def reduce_kernel(low, *refs):
    refs = list(refs)
    source = {name: refs.pop(0) for name in NAMES}
    emb_ref, one_ref, two_ref = refs.pop(0), refs.pop(0), refs.pop(0)
    out = {name: refs.pop(0) for name in ("qkv", "out", "up", "down", "head", "embed", "gain")}
    pool = refs
    grads, narrow, embed, local = pool.pop(0), pool.pop(0), pool.pop(0), pool.pop(0)
    partner, bits_of = neighbours(low)
    units = [narrow if name == "head" else grads.at[u if u < 9 else u - 1] for u, (name, _, _) in enumerate(UNITS)]
    copies = []
    for u, (name, part, _) in enumerate(UNITS):
        ref = source[name]
        if name == "down":
            ref = ref.at[:, :, :, :, part]
        elif name == "up":
            ref = ref.at[:, :, :, :, :, pl.ds(part * D, D)]
        copies.append(pltpu.make_async_copy(ref, units[u], local.at[u]))
    wide = emb_ref.shape[1]
    for half in range(2):
        copies.append(pltpu.make_async_copy(emb_ref.at[half], embed.at[half, pl.ds(0, wide)], local.at[len(UNITS) + half]))
    for copy in copies:
        copy.start()
    extra = jnp.concatenate([one_ref[:2], two_ref[:2], jnp.zeros((EMBED_ROWS - wide - 4, D), F32)], axis=0).astype(BF16)
    for half in range(2):
        embed[half, wide:] = extra
    meet(partner)

    def writer(name, part):
        def write(cols, value):
            if name == "head":
                out["head"][:, :] = value[:, : out["head"].shape[1]]
            elif name == "down":
                out["down"][pl.ds(part * ROWS, ROWS), cols] = value
            elif name == "out":
                out["out"][:, cols] = value
            else:
                first = part if name == "up" else "qkv".index(name)
                block = out["up" if name == "up" else "qkv"].at[:, pl.ds(first * D, D)]
                block[:, cols] = value

        return write

    def write_embed(cols, value):
        out["embed"][:, cols] = value[:wide]
        out["gain"][:, cols] = value[wide : wide + 8]

    jobs = []
    for u, (name, part, order) in enumerate(UNITS):
        jobs.append((copies[u : u + 1], unit_job(units[u], writer(name, part), order, unit_wide(name), partner, bits_of, pool)))
    jobs.append((copies[len(UNITS) :], embed_job(embed, write_embed, partner, bits_of, pool)))
    live = []
    for waits, job in jobs:
        for copy in waits:
            copy.wait()
        next(job)
        live.append(job)
    while live:
        live = [job for job in live if next(job, None) is not None]


def reduce_call(arrays, emb, gains_one, gains_two, low, wide):
    scratch = [
        pltpu.VMEM((len(UNITS) - 1, 2, 2, 2, 2, ROWS, D), BF16),
        pltpu.VMEM((2, 2, 2, 2, ROWS, NARROW), BF16),
        pltpu.VMEM((2, EMBED_ROWS, D), BF16),
        pltpu.SemaphoreType.DMA((len(UNITS) + 2,)),
    ]
    for name, _, order in UNITS:
        scratch += unit_scratch(order, unit_wide(name))
    scratch += embed_scratch()
    anywhere = pl.BlockSpec(memory_space=pl.ANY)
    sizes = [(ROWS, 3 * D), (ROWS, D), (ROWS, FF), (4 * ROWS, D), (ROWS, wide), (emb.shape[1], D), (8, D)]
    return pl.pallas_call(
        functools.partial(reduce_kernel, low),
        in_specs=[anywhere] * (len(NAMES) + 1) + [whole()] * 2,
        out_specs=[whole()] * 7,
        out_shape=[shape(size, F32) for size in sizes],
        scratch_shapes=scratch,
        compiler_params=params(collective_id=0, has_side_effects=True),
        name="reduce",
    )(*arrays, emb, gains_one, gains_two)


def per_device(toks, pixels, w_embed, w_qkv, w_out, w_up, w_down, w_head, first_gain, first_bias, second_gain, second_bias, patch_cells, field_ids, visible, cotangent):
    low = toks // SHARDS
    swap = lambda rows: lax.all_to_all(rows, "var", split_axis=0, concat_axis=1, tiled=True)
    back = lambda rows: lax.all_to_all(rows, "var", split_axis=1, concat_axis=0, tiled=True)
    pix = swap(pixels[0])
    cot = swap(cotangent[0])
    emb = lax.all_gather(w_embed, "var", axis=0, tiled=True)
    line = lambda vector: vector.reshape(1, D)
    start, normed, qkv = first_call(pix, patch_cells, emb, w_qkv, line(first_gain), line(first_bias))
    att, prob = attend_call(qkv, field_ids, visible)
    recon, act, n2, hid, final, down_in, branch, mid, attg, gains_two = middle_call(
        att, start, cot, w_out, w_up, w_down, w_head, line(second_gain), line(second_bias)
    )
    dq, dk, dv = attend_back_call(qkv, att, attg, prob)
    start_grad, pix_grad, gains_one = last_call(dq, dk, dv, start, mid, w_qkv, emb, line(first_gain))
    split = lambda grad: grad.reshape(2, 2, 2, 2, ROWS, -1)
    wide = cot.shape[1]
    arrays = [
        weight_call(act, down_in, "down_grad").reshape(2, 2, 2, 2, 4, ROWS, D),
        split(weight_call(n2, hid, "up_grad")),
        split(weight_call(att, branch, "out_grad")),
        split(weight_call(final, jnp.pad(cot, ((0, 0), (0, NARROW - wide))), "head_grad")),
    ] + [split(weight_call(normed, rows, "qkv_grad")) for rows in (dq, dk, dv)]
    emb_grad = weight_call(pix, start_grad, "embed_grad").reshape(2, -1, D)
    sums = reduce_call(arrays, emb_grad, gains_one, gains_two, low, wide)
    tok = lax.axis_index("tok")
    step = 1
    while step < low:
        pairs = [(i, i ^ step) for i in range(toks)]
        sums = [one + lax.ppermute(one.astype(BF16), "tok", pairs).astype(F32) for one in sums]
        step *= 2

    def cut(array):
        length = array.shape[0] // low
        return lax.dynamic_slice_in_dim(array, lax.rem(tok, low) * length, length, 0)

    qkv_sum, out_sum, up_sum, down_sum, head_sum = [cut(one) for one in sums[:5]]
    gain_sum = lax.dynamic_slice_in_dim(sums[6], tok * (D // toks), D // toks, 1)
    return (
        back(recon)[None],
        back(pix_grad)[None],
        sums[5],
        qkv_sum,
        out_sum,
        up_sum,
        down_sum,
        head_sum,
        gain_sum[0],
        gain_sum[1],
        gain_sum[2],
        gain_sum[3],
    )


def solution(mesh):
    rows = P("tok", None, "var")
    lines = P("tok", "var")
    in_specs = (rows, P("var", None)) + (P(),) * 9 + (lines,) * 3 + (rows,)
    out_specs = (rows, rows, P("var", None)) + (P("tok", None),) * 5 + (P("tok"),) * 4
    body = functools.partial(per_device, mesh.shape["tok"])
    return jax.shard_map(body, mesh=mesh, in_specs=in_specs, out_specs=out_specs, check_vma=False)
```

time: 893 us -> 304 us (0.34)
  waiting for transfers between devices: 427 us -> 15.5 us
  Pallas kernels: 0 us -> 236 us
  matrix products: 218 us -> 0 us
  other arithmetic: 80.4 us -> 0 us
  blocking collectives: 71 us -> 11.1 us
  local copies, waits for them, and re-layouts: 67.9 us -> 24.8 us
  between operations: 15.3 us -> 0.83 us
    reduce_scatter x6 -> x0, waiting for transfers between devices: 289 us -> none  [the longest x1 114 us: per_device(): lax.psum_scatter(down_grad, 'tok', scatter_dimension=0, tiled=True)]
    pallas_call x0 -> x14, Pallas kernels: none -> 236 us  [the longest x1 89.8 us: reduce_call(): pl.pallas_call(functools.partial(reduce_kernel, low), in_specs=[anywhere]...]
    dot_general x24 -> x0, matrix products: 218 us -> none  [the longest x6 50.3 us: dot_last(): lax.dot_general(left, right, (((1,), (1,)), ((), ())), preferred_element_...]
    psum x2 -> x0, waiting for transfers between devices: 121 us -> none  [the longest x1 88.5 us: per_device(): w_embed_grad = lax.psum(embed_weight, 'tok')]
    unnamed x1 -> x0, blocking collectives: 60.3 us -> none
    convert_element_type x17 -> x0, other arithmetic: 45 us -> none  [the longest x1 22.1 us: attention_backward(): score_grad = (probability * (prob_grad - row_dot)).astype(jnp.bfloat16)]
    reduce_sum x6 -> x0, other arithmetic: 18.6 us -> none  [the longest x1 11 us: attention_forward(): denominator = jnp.sum(lifted, axis=-1, keepdims=True)]
    unnamed x99 -> x37, local copies, waits for them, and re-layouts: 19.2 us -> 5.59 us
  transfers between devices with their start and end apart: 11 -> 4, of which waited for: 8 -> 2; matrix products, arithmetic and copies ran while one was open for 23% -> 4% of each run, Pallas kernels for 0% -> 54%
where the time goes in v1:
time: 304 us; the launch traced here: 303 us
  Pallas kernels  236 us (78%)
  local copies, waits for them, and re-layouts  24.8 us (8%)
  waiting for transfers between devices  15.5 us (5%)
  starting transfers between devices  15 us (5%)
  blocking collectives  11.1 us (4%)
    pallas_call x1, Pallas kernels, reduce_call(): pl.pallas_call(functools.partial(reduce_kernel, low), in_specs=[anywhere]...  89.8 us
    pallas_call x8, Pallas kernels, weight_call(): pl.pallas_call(weight_kernel, grid=(height // high, width // wide), in_sp...  42.4 us
    pallas_call x1, Pallas kernels, middle_call(): pl.pallas_call(middle_kernel, grid=(rows // TILE,), in_specs=[tile(D), ti...  40.4 us
    pallas_call x1, Pallas kernels, attend_call(): pl.pallas_call(attend_kernel, grid=(rows // BIG, pairs), in_specs=[block(...  20.1 us
    pallas_call x1, Pallas kernels, attend_back_call(): pl.pallas_call(attend_back_kernel, grid=(rows // BIG, pairs), in_specs=[b...  18.9 us
    pallas_call x1, Pallas kernels, last_call(): pl.pallas_call(last_kernel, grid=(rows // TILE,), in_specs=[tile(D)] * 5...  12.5 us
    pallas_call x1, Pallas kernels, first_call(): pl.pallas_call(first_kernel, grid=(rows // TILE,), in_specs=[tile(pix.sha...  12 us
    all_gather x1, blocking collectives, per_device(): emb = lax.all_gather(w_embed, 'var', axis=0, tiled=True)  11.1 us
  transfers between devices with their start and end apart: 4, of which 2 were waited for; matrix products, arithmetic and copies ran while one was open for 4% of the time, Pallas kernels for 54%

profile of v1, /device:TPU:0, one launch (start us, length us, event | category | flops | bytes accessed | tf_op | source)
XLA Modules:
  0.0 303.1 jit_solution(2148702688722631447)
XLA Ops:
  0.6 2.3 all_to_all.52
  4.0 4.2 %all-to-all-start = ((bf16[2,1024,160]{1,2,0:T(8,128)(2,1)}), bf16[2,1024,160]{1,2,0:T(8,128)(2,1)S(1)}, u32[]{:S(2)}, u32[]{:S(2)}) async-start(bf16[2,1024,160]{1,2,0:T(8,128)(2,1)} %copy.50), calls=%async_computation | async-start | bytes 1310720 | tf_op jit(solution)/shard_map/all_to_all | solution.py:556
  9.7 8.6 %all-to-all-done = bf16[2,1024,160]{1,2,0:T(8,128)(2,1)S(1)} async-done(((bf16[2,1024,160]{1,2,0:T(8,128)(2,1)}), bf16[2,1024,160]{1,2,0:T(8,128)(2,1)S(1)}, u32[]{:S(2)}, u32[]{:S(2)}) %all-to-all-start) | async-done | bytes 655392 | tf_op jit(solution)/shard_map/all_to_all | solution.py:556
  18.3 3.5 %all-to-all-start.1 = ((bf16[2,1024,160]{1,2,0:T(8,128)(2,1)}), bf16[2,1024,160]{1,2,0:T(8,128)(2,1)S(1)}, u32[]{:S(2)}, u32[]{:S(2)}) async-start(bf16[2,1024,160]{1,2,0:T(8,128)(2,1)} %copy.52), calls=%async_computation.1 | async-start | bytes 1310720 | tf_op jit(solution)/shard_map/all_to_all | solution.py:556
  25.3 11.1 %all_gather.3.emb_ref = bf16[320,768]{1,0:T(8,128)(2,1)} all-gather(bf16[160,768]{1,0:T(8,128)(2,1)S(1)} %copy-done.8), channel_id=1, replica_groups=mesh['var'=2,'tok'=16] {'var'}, dimensions={0}, use_global_device_ids=true | all-gather | bytes 737280 | tf_op jit(solution)/shard_map/all_gather | solution.py:560
  38.7 12.0 %first.1 = (f32[1024,768]{1,0:T(8,128)}, bf16[1024,768]{1,0:T(8,128)(2,1)}, bf16[1024,2304]{1,0:T(8,128)(2,1)}) custom-call(bf16[1024,320]{1,0:T(8,128)(2,1)} %copy.51.pix_ref.left_ref, s32[1,1024]{1,0:T(1,128)} %cell_ref.1, bf16[320,768]{1,0:T(8,128)(2,1)} %all_gather.3.emb_ref, bf16[768,2304]{1,0:T(8,128)(2,1)} %wqkv_ref.3, f32[1,768]{1,0:T(1,128)} %reshape.77.gain_ref, ...), custom_call_target="tpu_custom_call" | custom-call | tf_op jit(solution)/shard_map/first/pallas_call | solution.py:108
  50.7 20.1 %attend.1 = (bf16[1024,768]{1,0:T(8,128)(2,1)}, bf16[24,512,512]{2,1,0:T(8,128)(2,1)}) custom-call(bf16[1024,2304]{1,0:T(8,128)(2,1)} %get-tuple-element.40.q_ref.k_ref.v_ref, bf16[1024,2304]{1,0:T(8,128)(2,1)} %get-tuple-element.40.q_ref.k_ref.v_ref, bf16[1024,2304]{1,0:T(8,128)(2,1)} %get-tuple-element.40.q_ref.k_ref.v_ref, s32[1,1024]{1,0:T(1,128)} %id_ref.1, ...), custom_call_target="tpu_custom_call" | custom-call | tf_op jit(solution)/shard_map/attend/pallas_call | solution.py:153
  70.7 40.4 %middle.1 = (bf16[1024,320]{1,0:T(8,128)(2,1)}, bf16[1024,3072]{1,0:T(8,128)(2,1)}, bf16[1024,768]{1,0:T(8,128)(2,1)}, bf16[1024,3072]{1,0:T(8,128)(2,1)}, bf16[...) custom-call(bf16[1024,768]{1,0:T(8,128)(2,1)} %get-tuple-element.41., ...), custom_call_target="tpu_custom_call" | custom-call | tf_op jit(solution)/shard_map/middle/pallas_call | solution.py:218
  111.2 2.3 copy.55
  113.5 3.7 %all-to-all-start.2 = ((bf16[1024,2,160]{0,2,1:T(8,128)(2,1)}), bf16[1024,2,160]{0,2,1:T(8,128)(2,1)S(1)}, u32[]{:S(2)}, u32[]{:S(2)}) async-start(bf16[1024,2,160]{0,2,1:T(8,128)(2,1)} %bitcast.4), calls=%async_computation.2 | async-start | bytes 1310720 | tf_op jit(solution)/shard_map/all_to_all | solution.py:557
  118.2 4.3 %out_grad.1 = bf16[768,768]{1,0:T(8,128)(2,1)} custom-call(bf16[1024,768]{1,0:T(8,128)(2,1)} %get-tuple-element.41.att_ref.left_ref, bf16[1024,768]{1,0:T(8,128)(2,1)} %get-tuple-element.55.right_ref), custom_call_target="tpu_custom_call" | custom-call | tf_op jit(solution)/shard_map/out_grad/pallas_call | solution.py:313
  122.5 18.9 %attend_back.1 = (bf16[1024,768]{1,0:T(8,128)(2,1)}, bf16[1024,768]{1,0:T(8,128)(2,1)}, bf16[1024,768]{1,0:T(8,128)(2,1)}) custom-call(bf16[1024,2304]{1,0:T(8,128)(2,1)} %get-tuple-element.40.q_ref.k_ref.v_ref, bf16[1024,2304]{1,0:T(8,128)(2,1)} %get-tuple-element.40.q_ref.k_ref.v_ref, bf16[1024,2304]{1,0:T(8,128)(2,1)} %get-tuple-element.40.q_ref.k_ref.v_ref, ...), custom_call_target="tpu_custom_call" | custom-call | tf_op jit(solution)/shard_map/attend_back/pallas_call | solution.py:258
  141.4 4.3 %qkv_grad.5 = bf16[768,768]{1,0:T(8,128)(2,1)} custom-call(bf16[1024,768]{1,0:T(8,128)(2,1)} %get-tuple-element.57.left_ref, bf16[1024,768]{1,0:T(8,128)(2,1)} %get-tuple-element.48.dv_ref.right_ref), custom_call_target="tpu_custom_call" | custom-call | tf_op jit(solution)/shard_map/qkv_grad/pallas_call | solution.py:313
  145.7 4.3 %qkv_grad.4 = bf16[768,768]{1,0:T(8,128)(2,1)} custom-call(bf16[1024,768]{1,0:T(8,128)(2,1)} %get-tuple-element.57.left_ref, bf16[1024,768]{1,0:T(8,128)(2,1)} %get-tuple-element.47.dk_ref.right_ref), custom_call_target="tpu_custom_call" | custom-call | tf_op jit(solution)/shard_map/qkv_grad/pallas_call | solution.py:313
  150.1 4.3 %qkv_grad.3 = bf16[768,768]{1,0:T(8,128)(2,1)} custom-call(bf16[1024,768]{1,0:T(8,128)(2,1)} %get-tuple-element.57.left_ref, bf16[1024,768]{1,0:T(8,128)(2,1)} %get-tuple-element.46.dq_ref.right_ref), custom_call_target="tpu_custom_call" | custom-call | tf_op jit(solution)/shard_map/qkv_grad/pallas_call | solution.py:313
  154.4 12.5 %last.1 = (bf16[1024,768]{1,0:T(8,128)(2,1)}, bf16[1024,320]{1,0:T(8,128)(2,1)}, f32[8,768]{1,0:T(8,128)}) custom-call(bf16[1024,768]{1,0:T(8,128)(2,1)} %get-tuple-element.46.dq_ref.right_ref, bf16[1024,768]{1,0:T(8,128)(2,1)} %get-tuple-element.47.dk_ref.right_ref, bf16[1024,768]{1,0:T(8,128)(2,1)} %get-tuple-element.48.dv_ref.right_ref, ...), custom_call_target="tpu_custom_call" | custom-call | tf_op jit(solution)/shard_map/last/pallas_call | solution.py:293
  166.9 3.3 %embed_grad.1 = bf16[320,768]{1,0:T(8,128)(2,1)} custom-call(bf16[1024,320]{1,0:T(8,128)(2,1)} %copy.51.pix_ref.left_ref, bf16[1024,768]{1,0:T(8,128)(2,1)} %get-tuple-element.58.right_ref), custom_call_target="tpu_custom_call" | custom-call | tf_op jit(solution)/shard_map/embed_grad/pallas_call | solution.py:313
  171.2 3.4 %head_grad.1 = bf16[768,384]{1,0:T(8,128)(2,1)} custom-call(bf16[1024,768]{1,0:T(8,128)(2,1)} %get-tuple-element.56.left_ref, bf16[1024,384]{1,0:T(8,128)(2,1)} %pad.4.right_ref), custom_call_target="tpu_custom_call" | custom-call | tf_op jit(solution)/shard_map/head_grad/pallas_call | solution.py:313
  174.7 9.2 %down_grad.1 = bf16[3072,768]{1,0:T(8,128)(2,1)} custom-call(bf16[1024,3072]{1,0:T(8,128)(2,1)} %get-tuple-element.51.left_ref, bf16[1024,768]{1,0:T(8,128)(2,1)} %get-tuple-element.52.right_ref), custom_call_target="tpu_custom_call" | custom-call | tf_op jit(solution)/shard_map/down_grad/pallas_call | solution.py:313
  183.8 9.2 %up_grad.1 = bf16[768,3072]{1,0:T(8,128)(2,1)} custom-call(bf16[1024,768]{1,0:T(8,128)(2,1)} %get-tuple-element.53.left_ref, bf16[1024,3072]{1,0:T(8,128)(2,1)} %get-tuple-element.54.right_ref), custom_call_target="tpu_custom_call" | custom-call | tf_op jit(solution)/shard_map/up_grad/pallas_call | solution.py:313
  193.1 89.8 %reduce.1 = (f32[48,2304]{1,0:T(8,128)}, f32[48,768]{1,0:T(8,128)}, f32[48,3072]{1,0:T(8,128)}, f32[192,768]{1,0:T(8,128)}, f32[48,320]{1,0:T(8,128)}, /*index=5*/f32[160,768]{1,0:T(8,128)}, f32[8,768]{1,0:T(8,128)}) custom-call(bf16[2,2,2,2,4,48,768]{6,5,4,3,2,1,0:T(8,128)(2,1)} %bitcast.34, bf16[2,2,2,2,48,3072]{5,4,3,2,1,0:T(8,128)(2,1)} %bitcast.35, ...), custom_call_target="tpu_custom_call" | custom-call | tf_op jit(solution)/shard_map/reduce/pallas_call | solution.py:543
  282.9 3.5 %all-to-all-start.3 = ((bf16[1024,2,160]{0,2,1:T(8,128)(2,1)}), bf16[1024,2,160]{0,2,1:T(8,128)(2,1)S(1)}, u32[]{:S(2)}, u32[]{:S(2)}) async-start(bf16[1024,2,160]{0,2,1:T(8,128)(2,1)} %bitcast.6), calls=%async_computation.3 | async-start | bytes 1310720 | tf_op jit(solution)/shard_map/all_to_all | solution.py:557
  288.4 1.3 broadcast_in_dim.6
  289.7 6.9 %all-to-all-done.3 = bf16[1024,2,160]{0,2,1:T(8,128)(2,1)S(1)} async-done(((bf16[1024,2,160]{0,2,1:T(8,128)(2,1)}), bf16[1024,2,160]{0,2,1:T(8,128)(2,1)S(1)}, u32[]{:S(2)}, u32[]{:S(2)}) %all-to-all-start.3) | async-done | bytes 655392 | tf_op jit(solution)/shard_map/all_to_all | solution.py:557
  (55 shorter events, 18.8 us)
Async XLA Ops:
  3.0 5.2 %copy-start.2 = (bf16[1,2048,160]{1,2,0:T(8,128)(2,1)S(1)}, bf16[1,2048,160]{1,2,0:T(8,128)(2,1)}, u32[]{:S(2)}) copy-start(bf16[1,2048,160]{1,2,0:T(8,128)(2,1)} %param.29) | copy-start | bytes 1966084
  4.0 14.4 %all-to-all-start = ((bf16[2,1024,160]{1,2,0:T(8,128)(2,1)}), bf16[2,1024,160]{1,2,0:T(8,128)(2,1)S(1)}, u32[]{:S(2)}, u32[]{:S(2)}) async-start(bf16[2,1024,160]{1,2,0:T(8,128)(2,1)} %copy.50), calls=%async_computation | async-start | bytes 1310720 | tf_op jit(solution)/shard_map/all_to_all | solution.py:556
  8.7 13.2 %copy-start.11 = (f32[768]{0:T(1024)S(1)}, f32[768]{0:T(1024)}, u32[]{:S(2)}) copy-start(f32[768]{0:T(1024)} %param.22) | copy-start | bytes 9220
  8.7 13.8 %copy-start.12 = (f32[768]{0:T(1024)S(1)}, f32[768]{0:T(1024)}, u32[]{:S(2)}) copy-start(f32[768]{0:T(1024)} %param.23) | copy-start | bytes 9220
  8.7 14.3 %copy-start.13 = (f32[768]{0:T(1024)S(1)}, f32[768]{0:T(1024)}, u32[]{:S(2)}) copy-start(f32[768]{0:T(1024)} %param.24) | copy-start | bytes 9220
  8.7 14.9 %copy-start.14 = (f32[768]{0:T(1024)S(1)}, f32[768]{0:T(1024)}, u32[]{:S(2)}) copy-start(f32[768]{0:T(1024)} %param.25) | copy-start | bytes 9220
  8.7 15.5 %copy-start.5 = (bf16[768,320]{0,1:T(8,128)(2,1)S(1)}, bf16[768,320]{0,1:T(8,128)(2,1)}, u32[]{:S(2)}) copy-start(bf16[768,320]{0,1:T(8,128)(2,1)} %param.21) | copy-start | bytes 1474564
  8.7 16.5 %copy-start.8 = (bf16[160,768]{1,0:T(8,128)(2,1)S(1)}, bf16[160,768]{1,0:T(8,128)(2,1)}, u32[]{:S(2)}) copy-start(bf16[160,768]{1,0:T(8,128)(2,1)} %param.16) | copy-start | bytes 737284
  18.3 19.1 %all-to-all-start.1 = ((bf16[2,1024,160]{1,2,0:T(8,128)(2,1)}), bf16[2,1024,160]{1,2,0:T(8,128)(2,1)S(1)}, u32[]{:S(2)}, u32[]{:S(2)}) async-start(bf16[2,1024,160]{1,2,0:T(8,128)(2,1)} %copy.52), calls=%async_computation.1 | async-start | bytes 1310720 | tf_op jit(solution)/shard_map/all_to_all | solution.py:556
  111.1 6.1 %copy-start = (bf16[1024,320]{1,0:T(8,128)(2,1)S(1)}, bf16[1024,320]{1,0:T(8,128)(2,1)}, u32[]{:S(2)}) copy-start(bf16[1024,320]{1,0:T(8,128)(2,1)} %copy.53.cot_ref) | copy-start | bytes 1966084
  113.5 169.4 %all-to-all-start.2 = ((bf16[1024,2,160]{0,2,1:T(8,128)(2,1)}), bf16[1024,2,160]{0,2,1:T(8,128)(2,1)S(1)}, u32[]{:S(2)}, u32[]{:S(2)}) async-start(bf16[1024,2,160]{0,2,1:T(8,128)(2,1)} %bitcast.4), calls=%async_computation.2 | async-start | bytes 1310720 | tf_op jit(solution)/shard_map/all_to_all | solution.py:557
  166.8 3.3 %copy-start.1 = (bf16[1024,320]{1,0:T(8,128)(2,1)S(1)}, bf16[1024,320]{1,0:T(8,128)(2,1)}, u32[]{:S(2)}) copy-start(bf16[1024,320]{1,0:T(8,128)(2,1)} %get-tuple-element.50) | copy-start | bytes 1966084
  282.9 13.7 %all-to-all-start.3 = ((bf16[1024,2,160]{0,2,1:T(8,128)(2,1)}), bf16[1024,2,160]{0,2,1:T(8,128)(2,1)S(1)}, u32[]{:S(2)}, u32[]{:S(2)}) async-start(bf16[1024,2,160]{0,2,1:T(8,128)(2,1)} %bitcast.6), calls=%async_computation.3 | async-start | bytes 1310720 | tf_op jit(solution)/shard_map/all_to_all | solution.py:557
  289.7 8.9 %copy-start.6 = (f32[160,768]{1,0:T(8,128)S(1)}, f32[160,768]{1,0:T(8,128)}, u32[]{:S(2)}) copy-start(f32[160,768]{1,0:T(8,128)} %get-tuple-element.86) | copy-start | bytes 1474564
  296.6 2.8 copy-start.7
  297.2 2.9 copy-start.9
  297.3 3.6 %copy-start.4 = (f32[48,3072]{1,0:T(8,128)S(1)}, f32[48,3072]{1,0:T(8,128)}, u32[]{:S(2)}) copy-start(f32[48,3072]{1,0:T(8,128)} %get-tuple-element.89) | copy-start | bytes 1769476
  298.6 3.0 %copy-start.3 = (f32[192,768]{1,0:T(8,128)S(1)}, f32[192,768]{1,0:T(8,128)}, u32[]{:S(2)}) copy-start(f32[192,768]{1,0:T(8,128)} %get-tuple-element.90) | copy-start | bytes 1769476
  299.4 3.1 %copy-start.10 = (f32[48,320]{1,0:T(8,128)S(1)}, f32[48,320]{1,0:T(8,128)}, u32[]{:S(2)}) copy-start(f32[48,320]{1,0:T(8,128)} %get-tuple-element.91) | copy-start | bytes 184324
